TPU v7x, 256 devices: a whole 4x4x8 slice. The times are simulated.
256 devices in a mesh: member: 8 (over y, core), grid: 32 (over x, z).
Axes of the slice: x: 4, y: 4, z: 8, core: 2. Of those that a mesh axis runs over, the one named last changes fastest.
Arguments:
- predictions: float32 [8, 100, 32768], P('member', None, 'grid'), may hold values from -6 to 6
- truth: float32 [100, 32768], P(None, 'grid'), may hold values from -6 to 6
- area: float32 [32768], P('grid'), may hold values from 0.2 to 7.5
- queries: bfloat16 [4096, 1024], P('grid'), may hold values from -6 to 6
- cotangent: bfloat16 [8, 4096, 1024], P('member', 'grid'), may hold values from -6 to 6
- edge_slot: int32 [4096, 32], P('grid'), may hold values from 0 to 255, as said below
- edge_count: int32 [4096], P('grid'), may hold values from 2 to 32, as said below
- edge_bias: float32 [4096, 512], P('grid'), may hold values from -6 to 326
- send_rows: int32 [32, 32, 8], P('grid'), may hold values from 0 to 1023, as said below
- w_embed: bfloat16 [100, 1024], replicated, may hold values from -0.625 to 0.625
- w_query: bfloat16 [1024, 1024], replicated, may hold values from -0.1875 to 0.1875
- w_keyval: bfloat16 [1024, 2048], replicated, may hold values from -0.1875 to 0.1875
- w_out: bfloat16 [1024, 1024], replicated, may hold values from -0.1875 to 0.1875
Outputs:
- hidden: bfloat16 [8, 4096, 1024], P('member', 'grid')
- grad_pred: float32 [8, 100, 32768], P('member', None, 'grid')
- loss: float32 [], replicated
Inputs may be any that keep to these rules, and one draw needn't show every extreme that they name: `send_rows`: each sending tile names 8 rows for each owner; all rows a tile sends are distinct. `edge_slot`: slots of the owner's received rows; the slots of one node are distinct. `edge_count`: edges at or beyond a node's count are padding.
All inputs are finite; a program needn't handle non-finite values.
Results may differ from a plain program's by a relative error of at most 0.0089.
Values may be sent and summed in bfloat16 or wider, within the bound.
A program may use at most 64 MiB of HBM per device.

v0:
```python
import math

import jax
import jax.numpy as jnp
from jax import lax
from jax.sharding import PartitionSpec as P

alpha_fair = 0.95
big_negative = -1e30


def attend_owner(
    queries, key_val, edge_slot, edge_count, edge_bias, cotangent, w_query, w_keyval, w_out
):
    node_count, model_width = queries.shape
    edge_fan = edge_slot.shape[1]
    head_count = edge_bias.shape[1] // edge_fan
    head_size = model_width // head_count
    slot_count = key_val.shape[0]
    score_scale = 1.0 / math.sqrt(head_size)
    query_heads = jnp.dot(queries, w_query, preferred_element_type=jnp.float32).astype(jnp.bfloat16)
    query_heads = query_heads.reshape(node_count, head_count, head_size)
    key_heads = key_val[:, :model_width].reshape(slot_count, head_count, head_size)
    value_heads = key_val[:, model_width:].reshape(slot_count, head_count, head_size)
    active = jnp.arange(edge_fan)[None, :] < edge_count[:, None]
    chosen = jnp.logical_and(
        edge_slot[:, :, None] == jnp.arange(slot_count)[None, None, :], active[:, :, None]
    ).astype(jnp.float32)
    bias_full = jnp.einsum(
        "hks,hkn->hns",
        chosen,
        edge_bias.reshape(node_count, edge_fan, head_count),
        precision=lax.Precision.HIGHEST,
    )
    present = (jnp.sum(chosen, axis=1) > 0.5)[:, None, :]
    scores = (
        jnp.einsum("hnd,snd->hns", query_heads, key_heads, preferred_element_type=jnp.float32)
        * score_scale
        + bias_full
    )
    scores = jnp.where(present, scores, big_negative)
    row_top = jnp.max(scores, axis=-1, keepdims=True)
    exponent = jnp.where(present, jnp.exp(scores - row_top), 0.0)
    weights = exponent / jnp.sum(exponent, axis=-1, keepdims=True)
    weights_low = weights.astype(jnp.bfloat16)
    attended = jnp.einsum(
        "hns,snd->hnd", weights_low, value_heads, preferred_element_type=jnp.float32
    )
    attended = attended.astype(jnp.bfloat16).reshape(node_count, model_width)
    hidden = (
        queries.astype(jnp.float32) + jnp.dot(attended, w_out, preferred_element_type=jnp.float32)
    ).astype(jnp.bfloat16)
    grad_attended = lax.dot_general(
        cotangent, w_out, (((1,), (1,)), ((), ())), preferred_element_type=jnp.float32
    )
    grad_attended = grad_attended.astype(jnp.bfloat16).reshape(node_count, head_count, head_size)
    grad_weights = jnp.einsum(
        "hnd,snd->hns", grad_attended, value_heads, preferred_element_type=jnp.float32
    )
    inner = jnp.sum(weights * grad_weights, axis=-1, keepdims=True)
    grad_score = (weights * (grad_weights - inner) * score_scale).astype(jnp.bfloat16)
    grad_keys = jnp.einsum(
        "hns,hnd->snd", grad_score, query_heads, preferred_element_type=jnp.float32
    ).astype(jnp.bfloat16)
    grad_values = jnp.einsum(
        "hns,hnd->snd", weights_low, grad_attended, preferred_element_type=jnp.float32
    ).astype(jnp.bfloat16)
    grad_kv = jnp.concatenate(
        [grad_keys.reshape(slot_count, model_width), grad_values.reshape(slot_count, model_width)],
        axis=1,
    )
    slot_grad = lax.dot_general(
        grad_kv, w_keyval, (((1,), (1,)), ((), ())), preferred_element_type=jnp.float32
    ).astype(jnp.bfloat16)
    return (hidden, slot_grad)


def fair_coefficient(member_count):
    return alpha_fair / (2.0 * member_count * (member_count - 1)) + (1.0 - alpha_fair) / (
        2.0 * member_count * member_count
    )


def local(
    predictions,
    truth,
    area,
    queries,
    cotangent,
    edge_slot,
    edge_count,
    edge_bias,
    send_rows,
    w_embed,
    w_query,
    w_keyval,
    w_out,
):
    grid_count = lax.axis_size("grid")
    member_count = lax.axis_size("member")
    model_width = queries.shape[1]
    point_count = predictions.shape[2]
    variables = predictions.shape[1]
    capacity = send_rows.shape[2]
    own_pred = predictions[0]
    pred_low = own_pred.astype(jnp.bfloat16)
    sent_rows = send_rows[0].reshape(-1)
    embedded = lax.dot_general(
        pred_low, w_embed, (((0,), (0,)), ((), ())), preferred_element_type=jnp.float32
    ).astype(jnp.bfloat16)
    local_kv = jnp.dot(embedded, w_keyval, preferred_element_type=jnp.float32).astype(jnp.bfloat16)
    packed = local_kv[sent_rows].reshape(grid_count, capacity, 2 * model_width)
    received = lax.all_to_all(packed, "grid", split_axis=0, concat_axis=0, tiled=True)
    key_val = received.reshape(grid_count * capacity, 2 * model_width)
    hidden, slot_grad = attend_owner(
        queries, key_val, edge_slot, edge_count, edge_bias, cotangent[0], w_query, w_keyval, w_out
    )
    returned = lax.all_to_all(
        slot_grad.reshape(grid_count, capacity, model_width),
        "grid",
        split_axis=0,
        concat_axis=0,
        tiled=True,
    )
    returned = returned.reshape(grid_count * capacity, model_width)
    selector = (sent_rows[:, None] == jnp.arange(point_count)[None, :]).astype(jnp.bfloat16)
    grad_embedded = lax.dot_general(
        selector, returned, (((0,), (0,)), ((), ())), preferred_element_type=jnp.float32
    ).astype(jnp.bfloat16)
    encoder_grad = lax.dot_general(
        w_embed, grad_embedded, (((1,), (1,)), ((), ())), preferred_element_type=jnp.float32
    )
    coefficient = fair_coefficient(member_count)
    total_points = point_count * grid_count
    everyone = lax.all_gather(predictions, "member", axis=0, tiled=True)
    skill = jnp.mean(jnp.abs(everyone - truth[None]), axis=0)
    spread = jnp.sum(jnp.abs(everyone[:, None] - everyone[None, :]), axis=(0, 1))
    crps = skill - coefficient * spread
    total_loss, total_area = lax.psum((jnp.sum(area[None, :] * crps), jnp.sum(area)), "grid")
    slope = jnp.sign(own_pred - truth) / member_count - 2.0 * coefficient * jnp.sum(
        jnp.sign(own_pred[None] - everyone), axis=0
    )
    loss_grad = (area * total_points / total_area)[None, :] * slope
    loss = total_loss / (total_area * variables)
    grad_pred = loss_grad + encoder_grad
    return (hidden[None], grad_pred[None], loss)


def solution(mesh):
    return jax.shard_map(
        local,
        mesh=mesh,
        in_specs=(
            P("member", None, "grid"),
            P(None, "grid"),
            P("grid"),
            P("grid", None),
            P("member", "grid", None),
            P("grid", None),
            P("grid"),
            P("grid", None),
            P("grid", None, None),
            P(),
            P(),
            P(),
            P(),
        ),
        out_specs=(P("member", "grid", None), P("member", None, "grid"), P()),
        check_vma=False,
    )
```

profile of v0, /device:TPU:16, one launch (start us, length us, event | category | flops | bytes accessed | tf_op | source)
XLA Modules:
  0.0 195.2 jit_solution(3790498930154189459)
XLA Ops:
  7.2 2.0 %copy.91 = f32[1,100,1024]{2,1,0:T(8,128)} copy(f32[1,100,1024]{2,0,1:T(1,128)} %param.13) | data formatting | bytes 819200
  9.2 0.8 copy.62
  10.1 8.9 %convolution_convert_fusion = bf16[1024,2048]{1,0:T(8,128)(2,1)} fusion(bf16[1024,2048]{1,0:T(8,128)(2,1)} %param.24, bf16[100,1024]{1,0:T(8,128)(2,1)} %param.22, f32[1,100,1024]{2,0,1:T(1,128)} %param.13), kind=kOutput, calls=%fused_computation.8 | convolution fusion | flops 4507828224 | bytes 9003008 | tf_op jit(solution)/shard_map/dot_general | solution.py:111
  19.0 6.1 %gather_fusion = bf16[256,2048]{1,0:T(8,128)(2,1)} fusion(bf16[1024,2048]{1,0:T(8,128)(2,1)} %convolution_convert_fusion, s32[1024]{0:T(1024)S(1)} %pad_clamp_fusion), kind=kCustom, calls=%fused_computation | custom fusion | bytes 2098176 | tf_op jit(solution)/shard_map/gather | solution.py:112
  25.1 11.6 %all-to-all-start = ((bf16[32,8,2048]{2,1,0:T(8,128)(2,1)}), bf16[32,8,2048]{2,1,0:T(8,128)(2,1)S(1)}, u32[]{:S(2)}, u32[]{:S(2)}) async-start(bf16[32,8,2048]{2,1,0:T(8,128)(2,1)} %bitcast.1), calls=%async_computation | async-start | bytes 2097152 | tf_op jit(solution)/shard_map/all_to_all | solution.py:113
  37.6 1.5 convert_reduce_fusion
  39.2 1.1 copy.68
  40.3 1.4 copy.69
  41.7 4.6 %fusion.3 = f32[128,256,16]{1,2,0:T(8,128)} fusion(f32[128,32,16]{1,2,0:T(8,128)} %copy.69, s32[128,32]{1,0:T(8,128)S(1)} %copy.64, pred[128,32]{1,0:T(8,128)(4,1)S(1)} %iota_compare_fusion.4), kind=kOutput, calls=%fused_computation.7 | convolution fusion | flops 203423744 | bytes 2379776 | tf_op jit(solution)/shard_map/hks,hkn->hns/dot_general | solution.py:29
  46.3 3.0 %copy.70 = f32[128,256,16]{0,1,2:T(8,128)} copy(f32[128,256,16]{1,2,0:T(8,128)} %fusion.3) | data formatting | bytes 4194304 | tf_op jit(solution)/shard_map/hks,hkn->hns/dot_general | solution.py:29
  49.3 2.1 %convolution_convert_fusion.5 = bf16[128,1024]{1,0:T(8,128)(2,1)S(1)} fusion(bf16[128,1024]{1,0:T(8,128)(2,1)} %param.16, bf16[1024,1024]{1,0:T(8,128)(2,1)} %param.23), kind=kOutput, calls=%fused_computation.37 | convolution fusion | flops 268566528 | bytes 2621440 | tf_op jit(solution)/shard_map/dot_general | solution.py:21
  51.5 0.8 copy.67
  52.3 1.8 convolution_convert_fusion.3
  54.1 0.8 copy.74
  55.6 9.7 %all-to-all-done = bf16[32,8,2048]{2,1,0:T(8,128)(2,1)S(1)} async-done(((bf16[32,8,2048]{2,1,0:T(8,128)(2,1)}), bf16[32,8,2048]{2,1,0:T(8,128)(2,1)S(1)}, u32[]{:S(2)}, u32[]{:S(2)}) %all-to-all-start) | async-done | bytes 1048608 | tf_op jit(solution)/shard_map/all_to_all | solution.py:113
  65.2 1.1 fusion.53
  66.3 1.2 copy.63
  67.5 1.2 copy.66
  68.8 1.9 fusion.55
  70.7 4.0 %fusion.54 = (f32[128,16]{0,1:T(8,128)S(1)}, f32[128,16,256]{0,2,1:T(8,128)}) fusion(pred[128,256]{0,1:T(8,128)(4,1)S(1)} %copy.65, f32[128,256,16]{0,1,2:T(8,128)} %copy.70, bf16[256,16,64]{0,2,1:T(8,128)(2,1)S(1)} %bitcast.96, bf16[128,16,64]{0,2,1:T(8,128)(2,1)} %bitcast.97), kind=kOutput, calls=%fused_computation.66 | convolution fusion | flops 70254848 | bytes 5021696 | tf_op jit(solution)/shard_map/sub | solution.py:43
  74.7 4.3 %fusion.19 = bf16[16,64,256]{2,1,0:T(8,128)(2,1)S(1)} fusion(bf16[128,16,64]{0,2,1:T(8,128)(2,1)} %bitcast.98, f32[16,256,128]{2,1,0:T(8,128)} %fusion.55, f32[128,16,256]{0,2,1:T(8,128)} %get-tuple-element.24, f32[128,16]{0,1:T(8,128)S(1)} %get-tuple-element.23), kind=kOutput, calls=%fused_computation.27 | convolution fusion | flops 71043328 | bytes 4988928 | tf_op jit(solution)/shard_map/hns,hnd->snd/dot_general | solution.py:62
  79.0 2.2 %convolution_convert_fusion.1 = bf16[16,64,256]{2,1,0:T(8,128)(2,1)S(1)} fusion(bf16[128,16,64]{0,2,1:T(8,128)(2,1)S(1)} %bitcast.95, f32[128,16,256]{0,2,1:T(8,128)} %get-tuple-element.24, f32[128,16]{0,1:T(8,128)S(1)} %get-tuple-element.23), kind=kOutput, calls=%fused_computation.28 | convolution fusion | flops 68419584 | bytes 2891776 | tf_op jit(solution)/shard_map/hns,hnd->snd/dot_general | solution.py:65
  81.8 2.1 %fusion.20 = bf16[32,8,1024]{2,1,0:T(8,128)(2,1)} fusion(bf16[1024,2048]{1,0:T(8,128)(2,1)S(1)} %copy-done.13, bf16[256,1024]{0,1:T(8,128)(2,1)S(1)} %bitcast.102, bf16[256,1024]{0,1:T(8,128)(2,1)S(1)} %bitcast.101), kind=kOutput, calls=%fused_computation.30 | convolution fusion | flops 1076101120 | bytes 5767168 | tf_op jit(solution)/shard_map/dot_general | solution.py:72
  83.9 5.3 %all-to-all-start.1 = ((bf16[32,8,1024]{2,1,0:T(8,128)(2,1)}), bf16[32,8,1024]{2,1,0:T(8,128)(2,1)S(1)}, u32[]{:S(2)}, u32[]{:S(2)}) async-start(bf16[32,8,1024]{2,1,0:T(8,128)(2,1)} %fusion.20), calls=%async_computation.1 | async-start | bytes 1048576 | tf_op jit(solution)/shard_map/all_to_all | solution.py:118
  89.2 2.6 %convolution_convert_fusion.4 = bf16[16,64,128]{2,1,0:T(8,128)(2,1)} fusion(bf16[256,16,64]{0,2,1:T(8,128)(2,1)S(1)} %bitcast.92, f32[128,16,256]{0,2,1:T(8,128)} %get-tuple-element.24, f32[128,16]{0,1:T(8,128)S(1)} %get-tuple-element.23), kind=kOutput, calls=%fused_computation.36 | convolution fusion | flops 68288512 | bytes 2891776 | tf_op jit(solution)/shard_map/hns,snd->hnd/dot_general | solution.py:46
  91.8 4.0 %copy.77 = f32[8,100,1024]{2,0,1:T(8,128)S(1)} copy(f32[8,100,1024]{2,1,0:T(8,128)} %all-gather.2.cloned.1.call-done) | data formatting | bytes 6553600 | tf_op jit(solution)/shard_map/all_gather | solution.py:135
  95.9 4.4 %abs_reduce_fusion = f32[100,1024]{1,0:T(8,128)S(1)} fusion(f32[8,100,1024]{2,0,1:T(8,128)S(1)} %copy.77, f32[8,100,1024]{2,1,0:T(8,128)S(1)} %copy-done.1), kind=kLoop, calls=%fused_computation.3 | loop fusion | flops 19558400 | bytes 6963200 | tf_op jit(solution)/shard_map/reduce_sum | solution.py:137
  100.3 2.2 %abs_reduce_fusion.1 = (f32[100,1024]{1,0:T(8,128)S(1)}, f32[100,1024]{1,0:T(8,128)}) fusion(f32[8,100,1024]{2,1,0:T(8,128)S(1)} %copy-done.1, f32[100,1024]{1,0:T(8,128)S(1)} %copy-done.5, f32[100,1024]{1,0:T(8,128)S(1)} %bitcast.90), kind=kLoop, calls=%fused_computation.9 | loop fusion | flops 4710400 | bytes 4915200 | tf_op jit(solution)/shard_map/reduce_sum | solution.py:136
  103.2 1.2 fusion.31
  104.4 75.3 %all-reduce = (f32[]{:T(128)}, f32[]{:T(128)}) all-reduce(f32[]{:T(128)} %reduce_sum.74, f32[]{:T(128)} %multiply_reduce_fusion), channel_id=1, replica_groups=mesh['member'=8,'grid'=32] {'grid'}, use_global_device_ids=true, to_apply=%region_4.5 | all-reduce | flops 2 | bytes 16 | tf_op jit(solution)/shard_map/psum | solution.py:139
  180.4 3.3 %fusion.27 = f32[1,100,1024]{2,1,0:T(8,128)} fusion(bf16[100,1024]{1,0:T(8,128)(2,1)} %param.22, bf16[32,8,1024]{2,1,0:T(8,128)(2,1)S(1)} %all-to-all-done.1, s32[256]{0:T(256)S(1)} %copy-done.11, f32[100,1024]{1,0:T(8,128)} %get-tuple-element.16, f32[100,1024]{1,0:T(8,128)S(1)} %copy-done.5, f32[1024]{0:T(1024)S(1)} %multiply_divide_fusion, ...), kind=kOutput, calls=%fused_computation.34 | convolution fusion | flops 748613632 | bytes 2372608 | tf_op jit(solution)/shard_map/dot_general | solution.py:130
  183.7 2.2 %copy.78 = f32[1,100,1024]{2,0,1:T(1,128)} copy(f32[1,100,1024]{2,1,0:T(8,128)} %fusion.27) | data formatting | bytes 819200
  (43 shorter events, 3.7 us)
Async XLA Ops:
  7.2 45.2 %copy-start = (bf16[1024,1024]{1,0:T(8,128)(2,1)S(1)}, bf16[1024,1024]{1,0:T(8,128)(2,1)}, u32[]{:S(2)}) copy-start(bf16[1024,1024]{1,0:T(8,128)(2,1)} %param.25) | copy-start | bytes 6291460
  7.2 84.6 %all-gather.2.cloned.1.call-start = ((), (), s32[]{:S(2)}) async-start(), calls=%async_computation.2 | async-start | bytes 3833856 | tf_op jit(solution)/shard_map/all_gather | solution.py:135
  25.1 12.3 %copy-start.10 = (s32[128,32]{0,1:T(8,128)S(1)}, s32[128,32]{0,1:T(8,128)}, u32[]{:S(2)}) copy-start(s32[128,32]{0,1:T(8,128)} %param.18) | copy-start | bytes 49156
  25.1 12.4 %copy-start.12 = (s32[128]{0:T(128)S(1)}, s32[128]{0:T(128)}, u32[]{:S(2)}) copy-start(s32[128]{0:T(128)} %param.19) | copy-start | bytes 1540
  25.1 40.1 %all-to-all-start = ((bf16[32,8,2048]{2,1,0:T(8,128)(2,1)}), bf16[32,8,2048]{2,1,0:T(8,128)(2,1)S(1)}, u32[]{:S(2)}, u32[]{:S(2)}) async-start(bf16[32,8,2048]{2,1,0:T(8,128)(2,1)} %bitcast.1), calls=%async_computation | async-start | bytes 2097152 | tf_op jit(solution)/shard_map/all_to_all | solution.py:113
  51.5 3.5 %copy-start.8 = (f32[1024]{0:T(1024)S(1)}, f32[1024]{0:T(1024)}, u32[]{:S(2)}) copy-start(f32[1024]{0:T(1024)} %param.15) | copy-start | bytes 12292
  65.2 3.6 %copy-start.4 = (bf16[128,1024]{0,1:T(8,128)(2,1)S(1)}, bf16[128,1024]{0,1:T(8,128)(2,1)}, u32[]{:S(2)}) copy-start(bf16[128,1024]{0,1:T(8,128)(2,1)} %copy.74) | copy-start | bytes 786436
  79.0 2.8 %copy-start.13 = (bf16[1024,2048]{1,0:T(8,128)(2,1)S(1)}, bf16[1024,2048]{1,0:T(8,128)(2,1)}, u32[]{:S(2)}) copy-start(bf16[1024,2048]{1,0:T(8,128)(2,1)} %param.24) | copy-start | bytes 12582916
  83.9 96.5 %all-to-all-start.1 = ((bf16[32,8,1024]{2,1,0:T(8,128)(2,1)}), bf16[32,8,1024]{2,1,0:T(8,128)(2,1)S(1)}, u32[]{:S(2)}, u32[]{:S(2)}) async-start(bf16[32,8,1024]{2,1,0:T(8,128)(2,1)} %fusion.20), calls=%async_computation.1 | async-start | bytes 1048576 | tf_op jit(solution)/shard_map/all_to_all | solution.py:118
  91.8 4.0 %copy-start.1 = (f32[8,100,1024]{2,1,0:T(8,128)S(1)}, f32[8,100,1024]{2,1,0:T(8,128)}, u32[]{:S(2)}) copy-start(f32[8,100,1024]{2,1,0:T(8,128)} %all-gather.2.cloned.1.call-done) | copy-start | bytes 9830404
  95.8 4.5 %copy-start.2 = (f32[1,100,1024]{2,1,0:T(8,128)S(1)}, f32[1,100,1024]{2,1,0:T(8,128)}, u32[]{:S(2)}) copy-start(f32[1,100,1024]{2,1,0:T(8,128)} %copy.91) | copy-start | bytes 1228804
  95.8 4.5 %copy-start.5 = (f32[100,1024]{1,0:T(8,128)S(1)}, f32[100,1024]{1,0:T(8,128)}, u32[]{:S(2)}) copy-start(f32[100,1024]{1,0:T(8,128)} %param.14) | copy-start | bytes 1228804
  100.3 2.2 %copy-start.9 = (f32[1024]{0:T(1024)S(1)}, f32[1024]{0:T(1024)}, u32[]{:S(2)}) copy-start(f32[1024]{0:T(1024)} %param.15) | copy-start | bytes 12292
  100.3 2.9 %copy-start.3 = (bf16[128,1024]{1,0:T(8,128)(2,1)S(1)}, bf16[128,1024]{1,0:T(8,128)(2,1)}, u32[]{:S(2)}) copy-start(bf16[128,1024]{1,0:T(8,128)(2,1)} %param.16) | copy-start | bytes 786436
  100.3 2.9 %copy-start.7 = (bf16[16,64,128]{2,1,0:T(8,128)(2,1)S(1)}, bf16[16,64,128]{2,1,0:T(8,128)(2,1)}, u32[]{:S(2)}) copy-start(bf16[16,64,128]{2,1,0:T(8,128)(2,1)} %convolution_convert_fusion.4) | copy-start | bytes 786436
  102.5 77.9 %copy-start.6 = (f32[1,100,1024]{2,0,1:T(1,128)S(1)}, f32[1,100,1024]{2,0,1:T(1,128)}, u32[]{:S(2)}) copy-start(f32[1,100,1024]{2,0,1:T(1,128)} %param.13) | copy-start | bytes 1228804
  102.5 77.9 %copy-start.11 = (s32[256]{0:T(256)S(1)}, s32[256]{0:T(256)}, u32[]{:S(2)}) copy-start(s32[256]{0:T(256)} %eq.31) | copy-start | bytes 3076
Sparse Core Ops, SparseCore 0:
  9.8 32.8 all-gather.1
where the time goes:
time: 196 us; the launch traced here: 195 us
  blocking collectives  75.3 us (38%)
  matrix products  39 us (20%)
  local copies, waits for them, and re-layouts  27.4 us (14%)
  starting transfers between devices  17 us (9%)
  between operations  16.7 us (9%)
  other arithmetic  10.1 us (5%)
  waiting for transfers between devices  9.68 us (5%)
    psum x1, blocking collectives, local(): lax.psum((jnp.sum(area[None, :] * crps), jnp.sum(area)), 'grid')  75.3 us
    all_to_all x1, starting transfers between devices, local(): lax.all_to_all(packed, 'grid', split_axis=0, concat_axis=0, tiled=True)  11.6 us
    all_to_all x1, waiting for transfers between devices, local(): lax.all_to_all(packed, 'grid', split_axis=0, concat_axis=0, tiled=True)  9.66 us
    dot_general x1, matrix products, local(): jnp.dot(embedded, w_keyval, preferred_element_type=jnp.float32)  8.9 us
    unnamed x33, local copies, waits for them, and re-layouts  6.75 us
    gather x1, local copies, waits for them, and re-layouts, local(): packed = local_kv[sent_rows].reshape(grid_count, capacity, 2 * model_width)  6.1 us
    all_to_all x1, starting transfers between devices, local(): lax.all_to_all(slot_grad.reshape(grid_count, capacity, model_width), 'gri...  5.31 us
    dot_general x1, matrix products, attend_owner(): jnp.einsum('hks,hkn->hns', chosen, edge_bias.reshape(node_count, edge_fan...  4.61 us
  transfers between devices with their start and end apart: 3, of which 1 were waited for; matrix products, arithmetic and copies ran while one was open for 35% of the time, Pallas kernels for 0%

commit v1 on v0

v1 whole, which is shorter than its diff:
```python
import functools

import jax
import jax.numpy as jnp
from jax import lax
from jax.experimental import pallas as pl
from jax.experimental.pallas import tpu as pltpu
from jax.sharding import PartitionSpec as P

alpha_fair = 0.95
absent = -1e30
steep = 3e38

BF = jnp.bfloat16
F32 = jnp.float32
I32 = jnp.int32
LANES = 128
CHUNK = 32
GX, GZ = 4, 8


def dot(a, b, ca=1, cb=0):
    return lax.dot_general(a, b, (((ca,), (cb,)), ((), ())), preferred_element_type=F32)


def iota(shape, dim):
    return lax.broadcasted_iota(I32, shape, dim)


def lane_gather(x, idx):
    dims = lax.GatherDimensionNumbers(
        offset_dims=(),
        collapsed_slice_dims=(1,),
        start_index_map=(1,),
        operand_batching_dims=(0,),
        start_indices_batching_dims=(0,),
    )
    return lax.gather(
        x, idx[..., None], dims, (1, 1), mode=lax.GatherScatterMode.PROMISE_IN_BOUNDS
    )


def fair_coefficient(member_count):
    return alpha_fair / (2.0 * member_count * (member_count - 1)) + (1.0 - alpha_fair) / (
        2.0 * member_count * member_count
    )


def wait_bytes(ref, sem):
    pltpu.make_async_copy(ref, ref, sem).wait()


def kernel(
    grid_count,
    member_count,
    pred_h, truth_h, area_h, q_h, cot_h, es_h, ec_h, eb_h, sr_h, we_h, wq_h, wkv_h, wo_h,
    hid_o, base_o, recve, sel, loss_o,
    predl, truth, area, q, cot, es_t, ec, eb, sr, we, wq, wkv, wo,
    pred, predp, wep, sendx, recvx, sende, crecv, csend, cret, lsend, lrecv,
    bias, qb, qst, ast, ww, qw, qw_t, aw, aw_t, values, s_scr, g_scr, gs_scr, wts, att,
    ld_sem, own_sem, fs, fr, cs, cr, rs, rr, ls, lr, bs, br, ws, wr, qs, qr,
):
    G, M = grid_count, member_count
    gi = lax.axis_index("grid")
    mi = lax.axis_index("member")
    variables, points = pred.shape
    nodes, width = q.shape
    pairs = width // LANES
    slots = sendx.shape[0]
    cap = slots // G
    fan = es_t.shape[0]
    coefficient = fair_coefficient(M)

    core = lax.rem(mi, 2)
    partner = mi + 1 - 2 * core
    wq_h = wq_h.at[:, pl.ds(pl.multiple_of(core * (width // 2), LANES), width // 2)]
    wkv_h = wkv_h.at[:, pl.ds(pl.multiple_of(core * width, LANES), width)]
    sources = [sr_h, pred_h, area_h, we_h, es_h, ec_h, eb_h, wkv_h, q_h, wq_h, cot_h, wo_h, truth_h]
    targets = [sr, predl, area, we, es_t, ec, eb, wkv, q, wq, cot, wo, truth]
    loads = [
        pltpu.make_async_copy(s, t, ld_sem.at[i]) for i, (s, t) in enumerate(zip(sources, targets))
    ]
    for c in loads[:4]:
        c.start()

    barrier = pltpu.get_barrier_semaphore()

    def turn(index, k, count):
        moved = index + k
        return jnp.where(moved >= count, moved - count, moved)

    gx, gz = lax.div(gi, GZ), lax.rem(gi, GZ)
    steps = [(dx, dz) for dx in range(GX) for dz in range(GZ)][1:]
    steps.sort(key=lambda d: -(min(d[0], GX - d[0]) + min(d[1], GZ - d[1])))
    tiles = [turn(gx, dx, GX) * GZ + turn(gz, dz, GZ) for dx, dz in steps]
    for peer in tiles:
        pl.semaphore_signal(barrier, inc=1, device_id={"grid": peer})
    for k in range(1, M):
        pl.semaphore_signal(barrier, inc=1, device_id={"member": turn(mi, k, M)})
    for c in loads[4:]:
        c.start()

    loads[0].wait()
    spots = jnp.broadcast_to(sr[0].astype(F32)[None], (G, cap, G)).reshape(slots, G)
    pick = iota((slots, G), 1) == (iota((slots, G), 0) // cap)
    rows = jnp.sum(jnp.where(pick, spots, 0.0), axis=1, keepdims=True).astype(I32)
    for c in range(slots // 64):
        r = pl.ds(64 * c, 64)
        hit = iota((64, points), 1) == rows[64 * c : 64 * c + 64]
        sel[r, :] = jnp.where(hit, 1.0, 0.0).astype(BF)
    predp[...] = jnp.zeros_like(predp)
    wep[...] = jnp.zeros_like(wep)
    for c in loads[1:4]:
        c.wait()
    pred[...] = predl[:, 0, :]
    pl.semaphore_wait(barrier, G - 1 + M - 1)
    for k in range(1, M):
        peer = turn(mi, k, M)
        pltpu.make_async_remote_copy(
            src_ref=pred.at[:, pl.ds(pl.multiple_of(peer * LANES, LANES), LANES)],
            dst_ref=crecv.at[mi],
            send_sem=cs,
            recv_sem=cr,
            device_id={"member": peer},
        ).start()
    own_lanes = pl.ds(pl.multiple_of(mi * LANES, LANES), LANES)
    own_chunk = pltpu.make_async_copy(pred.at[:, own_lanes], crecv.at[mi], own_sem)
    own_chunk.start()
    predp[0:variables, :] = pred[...].astype(BF)
    tile_area = jnp.sum(area[...], axis=1, keepdims=True)
    lane = iota((slots, LANES), 1)
    sub = iota((slots, LANES), 0)
    x = dot(sel[...], predp[...], 1, 1)
    sendx[...] = jnp.where(lane == variables, tile_area, x)


    mine = pl.ds(pl.multiple_of(gi * cap, cap), cap)

    def send_grid(src, dst, s_sem, r_sem):
        for peer in tiles:
            theirs = pl.ds(pl.multiple_of(peer * cap, cap), cap)
            pltpu.make_async_remote_copy(
                src_ref=src.at[theirs],
                dst_ref=dst.at[mine],
                send_sem=s_sem,
                recv_sem=r_sem,
                device_id={"grid": peer},
            ).start()
        dst[mine, :] = src[mine, :]

    send_grid(sendx, recvx, fs, fr)

    for c in loads[4:]:
        c.wait()
    wep[0:variables, :] = we[...]
    real = iota((fan, nodes), 0) < ec[...]
    es = jnp.where(real, es_t[...], -1).astype(F32).T.astype(I32)

    def spread_bias(start):
        r = slice(start, start + CHUNK)
        edges = es[r, :]
        slot_ids = iota((CHUNK, slots), 1)
        inverse = jnp.full((CHUNK, slots), -1, I32)
        for e in range(fan):
            inverse = jnp.where(edges[:, e : e + 1] == slot_ids, e, inverse)
        there = inverse >= 0
        index = jnp.maximum(inverse, 0)
        columns = [eb[r, j * LANES : (j + 1) * LANES] for j in range(4)]
        l = iota((CHUNK, LANES), 1)
        edge = l & (fan - 1)
        for t in range(4):
            place = (edge & 7) * 16 + 4 * t + (l >> 5)
            table = lane_gather(columns[0], place)
            for j in range(1, 4):
                table = jnp.where((edge >> 3) == j, lane_gather(columns[j], place), table)
            for hh in range(4):
                h = 4 * t + hh
                rows_of = slice((h % 2) * nodes + start, (h % 2) * nodes + start + CHUNK)
                for side in range(slots // LANES):
                    cols = slice(side * LANES, (side + 1) * LANES)
                    got = lane_gather(table, index[:, cols] + 32 * hh)
                    bias[h // 2, rows_of, cols] = jnp.where(there[:, cols], got, absent)

    half = LANES // 2
    for stacked in (qst, ast):
        stacked[...] = jnp.zeros_like(stacked)

    def stack_heads(p, block, stacked):
        stacked[p, 0:nodes, 0:half] = block[:, 0:half]
        stacked[p, nodes:, half:] = block[:, half:]

    def hand_over(ref, s_sem, r_sem):
        return pltpu.make_async_remote_copy(
            src_ref=ref.at[core],
            dst_ref=ref.at[core],
            send_sem=s_sem,
            recv_sem=r_sem,
            device_id={"member": partner},
        )

    spread_bias(0)
    for c in range(width // 512):
        cols = slice(512 * c, 512 * c + 512)
        ww[core, :, cols] = dot(wep[...], wkv[:, cols]).astype(BF)
    hand_over(ww, ws, wr).start()
    spread_bias(CHUNK)
    qb[core] = (dot(q[...], wq[...]) * 0.125).astype(BF)
    hand_over(qb, qs, qr).start()
    for c in range(width // 512):
        cols = slice(512 * c, 512 * c + 512)
        grads = dot(cot[0], wo[cols, :], 1, 1).astype(BF)
        spread_bias((2 + c) * CHUNK)
        for k in range(4):
            stack_heads(4 * c + k, grads[:, k * LANES : (k + 1) * LANES], ast)
    wait_bytes(qb.at[0], qr)
    wait_bytes(ww.at[0], wr)
    for p in range(pairs):
        lanes = slice(p * LANES, (p + 1) * LANES)
        inner = slice((p % 4) * LANES, (p % 4 + 1) * LANES)
        stack_heads(p, qb[p // 4, :, inner], qst)
        for stacked, weights, by_node, by_field in (
            (qst, ww[0, :, lanes], qw, qw_t),
            (ast, ww[1, :, lanes], aw, aw_t),
        ):
            by_node[p] = dot(stacked[p], weights, 1, 1).astype(BF)
            by_field[p] = dot(weights, stacked[p], 1, 1).astype(BF)

    wait_bytes(recvx.at[pl.ds(0, slots - cap)], fr)
    received = recvx[...]
    first = (lane == variables) & ((sub & (cap - 1)) == 0)
    total_area = jnp.sum(
        jnp.sum(jnp.where(first, received, 0.0), axis=0, keepdims=True), axis=1, keepdims=True
    )
    fields_t = received.T.astype(BF)

    def products(p):
        s_scr[p] = dot(qw[p], fields_t)
        g_scr[p] = dot(aw[p], fields_t)

    enc = jnp.zeros((LANES, slots), F32)
    def statistics():
        own_chunk.wait()
        wait_bytes(crecv.at[pl.ds(0, M - 1)], cr)

        own_area = area[:, own_lanes]
        part = jnp.zeros((1, LANES), F32)
        csend[:, variables // 16 * 16 :, :] = jnp.zeros((M, 16, LANES), BF)
        for row in range(0, variables, 16):
            r = slice(row, min(row + 16, variables))
            fields = [crecv[j, r, :] for j in range(M)]
            fact = truth[r, own_lanes]
            ranks = [jnp.zeros_like(fact) for _ in range(M)]
            skill = jnp.zeros_like(fact)
            for j in range(M):
                skill += jnp.abs(fields[j] - fact)
                for k in range(j + 1, M):
                    s = jnp.clip((fields[j] - fields[k]) * steep, -1.0, 1.0)
                    ranks[j] += s
                    ranks[k] -= s
            spread = sum(ranks[j] * fields[j] for j in range(M))
            crps = skill / M - (2.0 * coefficient) * spread
            part += jnp.sum(own_area * crps, axis=0, keepdims=True)
            for j in range(M):
                csend[j, r, :] = ranks[j].astype(BF)
        lsend[...] = jnp.broadcast_to(jnp.sum(part, axis=1, keepdims=True), lsend.shape)
        for k in range(1, M):
            pltpu.make_async_remote_copy(
                src_ref=lsend,
                dst_ref=lrecv.at[mi],
                send_sem=ls,
                recv_sem=lr,
                device_id={"member": turn(mi, k, M)},
            ).start()
        lrecv[mi] = lsend[...]
        for k in range(1, M):
            peer = turn(mi, k, M)
            pltpu.make_async_remote_copy(
                src_ref=csend.at[peer],
                dst_ref=cret.at[mi],
                send_sem=rs,
                recv_sem=rr,
                device_id={"member": peer},
            ).start()
        cret[mi] = csend[mi]

    products(0)
    for p in range(pairs):
        if p == 2:
            statistics()
        if p + 1 < pairs:
            products(p + 1)
        for i in range(2):
            r = slice(i * nodes, (i + 1) * nodes)
            s = s_scr[p, r, :] + bias[p, r, :]
            e = jnp.exp(s - jnp.max(s, axis=1, keepdims=True))
            g = g_scr[p, r, :]
            share = 1.0 / jnp.sum(e, axis=1, keepdims=True)
            inner = jnp.sum(e * g, axis=1, keepdims=True) * share
            w = e * share
            wts[p, r, :] = w.astype(BF)
            gs_scr[p, r, :] = (w * (g - inner)).astype(BF)
        enc += dot(qw_t[p], gs_scr[p]) + dot(aw_t[p], wts[p])

    wait_bytes(lrecv.at[pl.ds(0, M - 1)], lr)
    tile_loss = jnp.sum(lrecv[:, 0, 0:1], axis=0, keepdims=True)
    sende[...] = jnp.where(lane == variables, tile_loss, enc.T)
    send_grid(sende, recve, bs, br)

    low = iota((nodes, LANES), 1) < half
    values[...] = dot(recvx[...].astype(BF), ww[1]).astype(BF)
    for p in range(pairs):
        both = dot(wts[p], values[:, p * LANES : (p + 1) * LANES])
        att[:, p * LANES : (p + 1) * LANES] = jnp.where(low, both[:nodes], both[nodes:]).astype(BF)
    hid_o[0] = (q[...].astype(F32) + dot(att[...], wo[...])).astype(BF)

    wait_bytes(cret.at[pl.ds(0, M - 1)], rr)
    scale = (points * G) / total_area
    for chunk in range(points // LANES):
        cols = slice(chunk * LANES, (chunk + 1) * LANES)
        d = pred[:, cols] - truth[:, cols]
        s = jnp.where(d > 0, 1.0, jnp.where(d < 0, -1.0, 0.0)) / M
        slope = s - (2.0 * coefficient) * cret[chunk, 0:variables, :].astype(F32)
        base_o[:, cols] = (area[:, cols] * scale) * slope

    wait_bytes(recve.at[pl.ds(0, slots - cap)], br)
    back = recve[...]
    total_loss = jnp.sum(
        jnp.sum(jnp.where(first, back, 0.0), axis=0, keepdims=True), axis=1, keepdims=True
    )
    loss_o[...] = total_loss / (total_area * variables)
    wait_bytes(sendx.at[pl.ds(0, slots - cap)], fs)
    wait_bytes(sende.at[pl.ds(0, slots - cap)], bs)
    wait_bytes(crecv.at[pl.ds(0, M - 1)], cs)
    wait_bytes(csend.at[pl.ds(0, M - 1)], rs)
    wait_bytes(lrecv.at[pl.ds(0, M - 1)], ls)
    wait_bytes(ww.at[0], ws)
    wait_bytes(qb.at[0], qs)


def finish(hid, base, recve, sel, loss, hid_o, grad_o, loss_o, grad, sems):
    variables, points = base.shape
    copies = [
        pltpu.make_async_copy(hid, hid_o, sems.at[0]),
        pltpu.make_async_copy(loss, loss_o, sems.at[1]),
    ]
    for c in copies:
        c.start()
    back = recve[...].T
    high = back.astype(BF)
    terms = jnp.concatenate([high, (back - high.astype(F32)).astype(BF)], axis=0)
    for c in range(points // 512):
        cols = slice(512 * c, 512 * c + 512)
        both = dot(terms, sel[:, cols])
        grad[:, 0, cols] = base[:, cols] + (both[:LANES] + both[LANES:])[:variables]
        copy = pltpu.make_async_copy(grad.at[:, :, cols], grad_o.at[:, :, cols], sems.at[2 + c])
        copy.start()
        copies.append(copy)
    for c in copies:
        c.wait()


def local(
    grid_count, member_count,
    predictions, truth, area, queries, cotangent, edge_slot, edge_count, edge_bias, send_rows,
    w_embed, w_query, w_keyval, w_out,
):
    G, M = grid_count, member_count
    variables, points = truth.shape
    nodes, width = queries.shape
    slots = send_rows.shape[1] * send_rows.shape[2]
    pairs = width // LANES
    area = area.reshape(1, points)
    edge_count = edge_count.reshape(1, nodes)
    predictions = jnp.transpose(predictions, (1, 0, 2))
    edge_slot = edge_slot.T
    send_rows = jnp.transpose(send_rows, (0, 2, 1))
    args = (
        predictions, truth, area, queries, cotangent, edge_slot, edge_count, edge_bias, send_rows,
        w_embed, w_query, w_keyval, w_out,
    )
    args = tuple(pltpu.with_memory_space_constraint(a, pltpu.HBM) for a in args)
    rank_rows = (variables + 15) // 16 * 16
    hbm_spec = pl.BlockSpec(memory_space=pltpu.HBM)
    vmem_spec = pl.BlockSpec(memory_space=pltpu.VMEM)
    vm = pltpu.VMEM
    dma = pltpu.SemaphoreType.DMA
    shapes = [a.shape for a in args]
    shapes[10] = (width, width // 2)
    shapes[11] = (width, width)
    parts = pl.pallas_call(
        functools.partial(kernel, G, M),
        out_shape=(
            vm((1, nodes, width), BF),
            vm((variables, points), F32),
            vm((slots, LANES), F32),
            vm((slots, points), BF),
            vm((1, 1), F32),
        ),
        in_specs=[hbm_spec] * len(args),
        out_specs=(vmem_spec,) * 5,
        scratch_shapes=[vm(shape, a.dtype) for shape, a in zip(shapes, args)]
        + [
            vm((variables, points), F32),
            vm((LANES, points), BF),
            vm((LANES, width), BF),
            vm((slots, LANES), F32),
            vm((slots, LANES), F32),
            vm((slots, LANES), F32),
            vm((M, variables, LANES), F32),
            vm((M, rank_rows, LANES), BF),
            vm((M, rank_rows, LANES), BF),
            vm((8, LANES), F32),
            vm((M, 8, LANES), F32),
            vm((pairs, 2 * nodes, slots), F32),
            vm((2, nodes, width // 2), BF),
            vm((pairs, 2 * nodes, LANES), BF),
            vm((pairs, 2 * nodes, LANES), BF),
            vm((2, LANES, width), BF),
            vm((pairs, 2 * nodes, LANES), BF),
            vm((pairs, LANES, 2 * nodes), BF),
            vm((pairs, 2 * nodes, LANES), BF),
            vm((pairs, LANES, 2 * nodes), BF),
            vm((slots, width), BF),
            vm((pairs, 2 * nodes, slots), F32),
            vm((pairs, 2 * nodes, slots), F32),
            vm((pairs, 2 * nodes, slots), BF),
            vm((pairs, 2 * nodes, slots), BF),
            vm((nodes, width), BF),
            dma((len(args),)),
            *([dma] * 15),
        ],
        compiler_params=pltpu.CompilerParams(
            collective_id=0, has_side_effects=True, vmem_limit_bytes=48 * 1024 * 1024
        ),
    )(*args)
    hidden, grad_pred, loss = pl.pallas_call(
        finish,
        out_shape=(
            jax.ShapeDtypeStruct((1, nodes, width), BF),
            jax.ShapeDtypeStruct((variables, 1, points), F32),
            jax.ShapeDtypeStruct((1, 1), F32),
        ),
        in_specs=[vmem_spec] * 5,
        out_specs=(hbm_spec,) * 3,
        scratch_shapes=[vm((variables, 1, points), F32), dma((4,))],
        compiler_params=pltpu.CompilerParams(vmem_limit_bytes=16 * 1024 * 1024),
    )(*parts)
    return hidden, jnp.transpose(grad_pred, (1, 0, 2)), loss.reshape(())


def solution(mesh):
    return jax.shard_map(
        functools.partial(local, mesh.shape["grid"], mesh.shape["member"]),
        mesh=mesh,
        in_specs=(
            P("member", None, "grid"),
            P(None, "grid"),
            P("grid"),
            P("grid", None),
            P("member", "grid", None),
            P("grid", None),
            P("grid"),
            P("grid", None),
            P("grid", None, None),
            P(),
            P(),
            P(),
            P(),
        ),
        out_specs=(P("member", "grid", None), P("member", None, "grid"), P()),
        check_vma=False,
    )
```

time: 196 us -> 33.3 us (0.17)
  the two profiles are of different devices: /device:TPU:16 before, /device:TPU:1 now
where the time goes in v1:
time: 33.3 us; the launch traced here: 33.2 us
  Pallas kernels  32.5 us (98%)
  between operations  0.64 us (2%)
    pallas_call x1, Pallas kernels, local(): pl.pallas_call(functools.partial(kernel, G, M), out_shape=(vm((1, nodes,...  30.8 us
    pallas_call x1, Pallas kernels, local(): pl.pallas_call(finish, out_shape=(jax.ShapeDtypeStruct((1, nodes, width),...  1.71 us

profile of v1, /device:TPU:1, one launch (start us, length us, event | category | flops | bytes accessed | tf_op | source)
XLA Modules:
  0.0 33.2 jit_solution(1132668745375150185)
XLA Ops:
  0.6 30.8 %shard_map.148 = (bf16[1,128,1024]{2,1,0:T(8,128)(2,1)S(1)}, f32[100,1024]{1,0:T(8,128)S(1)}, f32[256,128]{1,0:T(8,128)S(1)}, bf16[256,1024]{1,0:T(8,128)(2,1)S(1)}, f32[1,1]{1,0:T(1,128)}) custom-call(f32[100,1,1024]{2,1,0:T(1,128)} %bitcast.7, f32[100,1024]{1,0:T(8,128)} %truth_h.1, f32[1,1024]{1,0:T(1,128)} %bitcast.9, bf16[128,1024]{1,0:T(8,128)(2,1)} %q_h.1, ...), custom_call_target="tpu_custom_call" | custom-call | tf_op jit(solution)/shard_map/pallas_call | solution.py:390
  31.5 1.7 %shard_map.149 = (bf16[1,128,1024]{2,1,0:T(8,128)(2,1)}, f32[100,1,1024]{2,1,0:T(1,128)}, f32[1,1]{1,0:T(1,128)}) custom-call(bf16[1,128,1024]{2,1,0:T(8,128)(2,1)S(1)} %get-tuple-element.11.hid, f32[100,1024]{1,0:T(8,128)S(1)} %get-tuple-element.12.base, f32[256,128]{1,0:T(8,128)S(1)} %get-tuple-element.13.recve, ...), custom_call_target="tpu_custom_call" | custom-call | tf_op jit(solution)/shard_map/pallas_call | solution.py:436

commit v2 on v1

--- a/solution.py
+++ b/solution.py
@@ -54,7 +54,7 @@
     grid_count,
     member_count,
     pred_h, truth_h, area_h, q_h, cot_h, es_h, ec_h, eb_h, sr_h, we_h, wq_h, wkv_h, wo_h,
-    hid_o, base_o, recve, sel, loss_o,
+    hid_o, base_o, recve, sel, area_o,
     predl, truth, area, q, cot, es_t, ec, eb, sr, we, wq, wkv, wo,
     pred, predp, wep, sendx, recvx, sende, crecv, csend, cret, lsend, lrecv,
     bias, qb, qst, ast, ww, qw, qw_t, aw, aw_t, values, s_scr, g_scr, gs_scr, wts, att,
@@ -75,8 +75,8 @@
     partner = mi + 1 - 2 * core
     wq_h = wq_h.at[:, pl.ds(pl.multiple_of(core * (width // 2), LANES), width // 2)]
     wkv_h = wkv_h.at[:, pl.ds(pl.multiple_of(core * width, LANES), width)]
-    sources = [sr_h, pred_h, area_h, we_h, es_h, ec_h, eb_h, wkv_h, q_h, wq_h, cot_h, wo_h, truth_h]
-    targets = [sr, predl, area, we, es_t, ec, eb, wkv, q, wq, cot, wo, truth]
+    sources = [sr_h, pred_h, area_h, we_h, wkv_h, q_h, wq_h, es_h, ec_h, eb_h, cot_h, wo_h, truth_h]
+    targets = [sr, predl, area, we, wkv, q, wq, es_t, ec, eb, cot, wo, truth]
     loads = [
         pltpu.make_async_copy(s, t, ld_sem.at[i]) for i, (s, t) in enumerate(zip(sources, targets))
     ]
@@ -113,7 +113,52 @@
     for c in loads[1:4]:
         c.wait()
     pred[...] = predl[:, 0, :]
+    predp[0:variables, :] = pred[...].astype(BF)
+    tile_area = jnp.sum(area[...], axis=1, keepdims=True)
+    lane = iota((slots, LANES), 1)
+    sub = iota((slots, LANES), 0)
+    x = dot(sel[...], predp[...], 1, 1)
+    sendx[...] = jnp.where(lane == variables, tile_area, x)
+
+
+    for c in loads[4:7]:
+        c.wait()
+    wep[0:variables, :] = we[...]
+    for c in range(width // 512):
+        cols = slice(512 * c, 512 * c + 512)
+        ww[core, :, cols] = dot(wep[...], wkv[:, cols]).astype(BF)
+    qb[core] = (dot(q[...], wq[...]) * 0.125).astype(BF)
+
     pl.semaphore_wait(barrier, G - 1 + M - 1)
+
+    def hand_over(ref, s_sem, r_sem):
+        return pltpu.make_async_remote_copy(
+            src_ref=ref.at[core],
+            dst_ref=ref.at[core],
+            send_sem=s_sem,
+            recv_sem=r_sem,
+            device_id={"member": partner},
+        )
+
+    hand_over(ww, ws, wr).start()
+    hand_over(qb, qs, qr).start()
+
+    mine = pl.ds(pl.multiple_of(gi * cap, cap), cap)
+
+    def send_grid(src, dst, s_sem, r_sem):
+        for peer in tiles:
+            theirs = pl.ds(pl.multiple_of(peer * cap, cap), cap)
+            pltpu.make_async_remote_copy(
+                src_ref=src.at[theirs],
+                dst_ref=dst.at[mine],
+                send_sem=s_sem,
+                recv_sem=r_sem,
+                device_id={"grid": peer},
+            ).start()
+        dst[mine, :] = src[mine, :]
+
+    send_grid(sendx, recvx, fs, fr)
+
     for k in range(1, M):
         peer = turn(mi, k, M)
         pltpu.make_async_remote_copy(
@@ -126,33 +171,9 @@
     own_lanes = pl.ds(pl.multiple_of(mi * LANES, LANES), LANES)
     own_chunk = pltpu.make_async_copy(pred.at[:, own_lanes], crecv.at[mi], own_sem)
     own_chunk.start()
-    predp[0:variables, :] = pred[...].astype(BF)
-    tile_area = jnp.sum(area[...], axis=1, keepdims=True)
-    lane = iota((slots, LANES), 1)
-    sub = iota((slots, LANES), 0)
-    x = dot(sel[...], predp[...], 1, 1)
-    sendx[...] = jnp.where(lane == variables, tile_area, x)
-
-
-    mine = pl.ds(pl.multiple_of(gi * cap, cap), cap)
-
-    def send_grid(src, dst, s_sem, r_sem):
-        for peer in tiles:
-            theirs = pl.ds(pl.multiple_of(peer * cap, cap), cap)
-            pltpu.make_async_remote_copy(
-                src_ref=src.at[theirs],
-                dst_ref=dst.at[mine],
-                send_sem=s_sem,
-                recv_sem=r_sem,
-                device_id={"grid": peer},
-            ).start()
-        dst[mine, :] = src[mine, :]
-
-    send_grid(sendx, recvx, fs, fr)
-
-    for c in loads[4:]:
+
+    for c in loads[7:]:
         c.wait()
-    wep[0:variables, :] = we[...]
     real = iota((fan, nodes), 0) < ec[...]
     es = jnp.where(real, es_t[...], -1).astype(F32).T.astype(I32)
 
@@ -189,27 +210,11 @@
         stacked[p, 0:nodes, 0:half] = block[:, 0:half]
         stacked[p, nodes:, half:] = block[:, half:]
 
-    def hand_over(ref, s_sem, r_sem):
-        return pltpu.make_async_remote_copy(
-            src_ref=ref.at[core],
-            dst_ref=ref.at[core],
-            send_sem=s_sem,
-            recv_sem=r_sem,
-            device_id={"member": partner},
-        )
-
-    spread_bias(0)
-    for c in range(width // 512):
-        cols = slice(512 * c, 512 * c + 512)
-        ww[core, :, cols] = dot(wep[...], wkv[:, cols]).astype(BF)
-    hand_over(ww, ws, wr).start()
-    spread_bias(CHUNK)
-    qb[core] = (dot(q[...], wq[...]) * 0.125).astype(BF)
-    hand_over(qb, qs, qr).start()
     for c in range(width // 512):
         cols = slice(512 * c, 512 * c + 512)
         grads = dot(cot[0], wo[cols, :], 1, 1).astype(BF)
-        spread_bias((2 + c) * CHUNK)
+        spread_bias(2 * c * CHUNK)
+        spread_bias((2 * c + 1) * CHUNK)
         for k in range(4):
             stack_heads(4 * c + k, grads[:, k * LANES : (k + 1) * LANES], ast)
     wait_bytes(qb.at[0], qr)
@@ -285,7 +290,7 @@
 
     products(0)
     for p in range(pairs):
-        if p == 2:
+        if p == 5:
             statistics()
         if p + 1 < pairs:
             products(p + 1)
@@ -314,6 +319,7 @@
     hid_o[0] = (q[...].astype(F32) + dot(att[...], wo[...])).astype(BF)
 
     wait_bytes(cret.at[pl.ds(0, M - 1)], rr)
+    area_o[...] = total_area
     scale = (points * G) / total_area
     for chunk in range(points // LANES):
         cols = slice(chunk * LANES, (chunk + 1) * LANES)
@@ -323,11 +329,6 @@
         base_o[:, cols] = (area[:, cols] * scale) * slope
 
     wait_bytes(recve.at[pl.ds(0, slots - cap)], br)
-    back = recve[...]
-    total_loss = jnp.sum(
-        jnp.sum(jnp.where(first, back, 0.0), axis=0, keepdims=True), axis=1, keepdims=True
-    )
-    loss_o[...] = total_loss / (total_area * variables)
     wait_bytes(sendx.at[pl.ds(0, slots - cap)], fs)
     wait_bytes(sende.at[pl.ds(0, slots - cap)], bs)
     wait_bytes(crecv.at[pl.ds(0, M - 1)], cs)
@@ -337,14 +338,10 @@
     wait_bytes(qb.at[0], qs)
 
 
-def finish(hid, base, recve, sel, loss, hid_o, grad_o, loss_o, grad, sems):
+def finish(cap, hid, base, recve, sel, area, hid_o, grad_o, loss_o, grad, loss, sems):
     variables, points = base.shape
-    copies = [
-        pltpu.make_async_copy(hid, hid_o, sems.at[0]),
-        pltpu.make_async_copy(loss, loss_o, sems.at[1]),
-    ]
-    for c in copies:
-        c.start()
+    copies = [pltpu.make_async_copy(hid, hid_o, sems.at[0])]
+    copies[0].start()
     back = recve[...].T
     high = back.astype(BF)
     terms = jnp.concatenate([high, (back - high.astype(F32)).astype(BF)], axis=0)
@@ -355,7 +352,13 @@
         copy = pltpu.make_async_copy(grad.at[:, :, cols], grad_o.at[:, :, cols], sems.at[2 + c])
         copy.start()
         copies.append(copy)
-    for c in copies:
+    back = recve[...]
+    first = (iota(back.shape, 1) == variables) & ((iota(back.shape, 0) & (cap - 1)) == 0)
+    total = jnp.sum(jnp.where(first, back, 0.0), axis=0, keepdims=True)
+    loss[...] = jnp.sum(total, axis=1, keepdims=True) / (area[...] * variables)
+    copy = pltpu.make_async_copy(loss, loss_o, sems.at[1])
+    copy.start()
+    for c in copies + [copy]:
         c.wait()
 
 
@@ -434,7 +437,7 @@
         ),
     )(*args)
     hidden, grad_pred, loss = pl.pallas_call(
-        finish,
+        functools.partial(finish, slots // G),
         out_shape=(
             jax.ShapeDtypeStruct((1, nodes, width), BF),
             jax.ShapeDtypeStruct((variables, 1, points), F32),
@@ -442,7 +445,7 @@
         ),
         in_specs=[vmem_spec] * 5,
         out_specs=(hbm_spec,) * 3,
-        scratch_shapes=[vm((variables, 1, points), F32), dma((4,))],
+        scratch_shapes=[vm((variables, 1, points), F32), vm((1, 1), F32), dma((4,))],
         compiler_params=pltpu.CompilerParams(vmem_limit_bytes=16 * 1024 * 1024),
     )(*parts)
     return hidden, jnp.transpose(grad_pred, (1, 0, 2)), loss.reshape(())

time: 33.3 us -> 33.2 us (level)
  no operation moved by 1% of the time
where the time goes in v2:
time: 33.2 us; the launch traced here: 33.1 us
  Pallas kernels  32.4 us (98%)
  between operations  0.64 us (2%)
    pallas_call x1, Pallas kernels, local(): pl.pallas_call(functools.partial(kernel, G, M), out_shape=(vm((1, nodes,...  30.7 us
    pallas_call x1, Pallas kernels, local(): pl.pallas_call(functools.partial(finish, slots // G), out_shape=(jax.Shap...  1.71 us

profile of v2, /device:TPU:1, one launch (start us, length us, event | category | flops | bytes accessed | tf_op | source)
XLA Modules:
  0.0 33.1 jit_solution(4949517820564450226)
XLA Ops:
  0.6 30.7 %shard_map.148 = (bf16[1,128,1024]{2,1,0:T(8,128)(2,1)S(1)}, f32[100,1024]{1,0:T(8,128)S(1)}, f32[256,128]{1,0:T(8,128)S(1)}, bf16[256,1024]{1,0:T(8,128)(2,1)S(1)}, f32[1,1]{1,0:T(1,128)}) custom-call(f32[100,1,1024]{2,1,0:T(1,128)} %bitcast.7, f32[100,1024]{1,0:T(8,128)} %truth_h.1, f32[1,1024]{1,0:T(1,128)} %bitcast.9, bf16[128,1024]{1,0:T(8,128)(2,1)} %q_h.1, ...), custom_call_target="tpu_custom_call" | custom-call | tf_op jit(solution)/shard_map/pallas_call | solution.py:393
  31.3 1.7 %shard_map.149 = (bf16[1,128,1024]{2,1,0:T(8,128)(2,1)}, f32[100,1,1024]{2,1,0:T(1,128)}, f32[1,1]{1,0:T(1,128)}) custom-call(bf16[1,128,1024]{2,1,0:T(8,128)(2,1)S(1)} %get-tuple-element.11.hid, f32[100,1024]{1,0:T(8,128)S(1)} %get-tuple-element.12.base, f32[256,128]{1,0:T(8,128)S(1)} %get-tuple-element.13.recve, ...), custom_call_target="tpu_custom_call" | custom-call | tf_op jit(solution)/shard_map/pallas_call | solution.py:439

commit v3 on v2

--- a/solution.py
+++ b/solution.py
@@ -75,8 +75,8 @@
     partner = mi + 1 - 2 * core
     wq_h = wq_h.at[:, pl.ds(pl.multiple_of(core * (width // 2), LANES), width // 2)]
     wkv_h = wkv_h.at[:, pl.ds(pl.multiple_of(core * width, LANES), width)]
-    sources = [sr_h, pred_h, area_h, we_h, wkv_h, q_h, wq_h, es_h, ec_h, eb_h, cot_h, wo_h, truth_h]
-    targets = [sr, predl, area, we, wkv, q, wq, es_t, ec, eb, cot, wo, truth]
+    sources = [sr_h, pred_h, area_h, we_h, es_h, ec_h, eb_h, q_h, wkv_h, wq_h, cot_h, wo_h, truth_h]
+    targets = [sr, predl, area, we, es_t, ec, eb, q, wkv, wq, cot, wo, truth]
     loads = [
         pltpu.make_async_copy(s, t, ld_sem.at[i]) for i, (s, t) in enumerate(zip(sources, targets))
     ]
@@ -110,8 +110,9 @@
         sel[r, :] = jnp.where(hit, 1.0, 0.0).astype(BF)
     predp[...] = jnp.zeros_like(predp)
     wep[...] = jnp.zeros_like(wep)
-    for c in loads[1:4]:
+    for c in loads[1:10]:
         c.wait()
+    wep[0:variables, :] = we[...]
     pred[...] = predl[:, 0, :]
     predp[0:variables, :] = pred[...].astype(BF)
     tile_area = jnp.sum(area[...], axis=1, keepdims=True)
@@ -121,59 +122,6 @@
     sendx[...] = jnp.where(lane == variables, tile_area, x)
 
 
-    for c in loads[4:7]:
-        c.wait()
-    wep[0:variables, :] = we[...]
-    for c in range(width // 512):
-        cols = slice(512 * c, 512 * c + 512)
-        ww[core, :, cols] = dot(wep[...], wkv[:, cols]).astype(BF)
-    qb[core] = (dot(q[...], wq[...]) * 0.125).astype(BF)
-
-    pl.semaphore_wait(barrier, G - 1 + M - 1)
-
-    def hand_over(ref, s_sem, r_sem):
-        return pltpu.make_async_remote_copy(
-            src_ref=ref.at[core],
-            dst_ref=ref.at[core],
-            send_sem=s_sem,
-            recv_sem=r_sem,
-            device_id={"member": partner},
-        )
-
-    hand_over(ww, ws, wr).start()
-    hand_over(qb, qs, qr).start()
-
-    mine = pl.ds(pl.multiple_of(gi * cap, cap), cap)
-
-    def send_grid(src, dst, s_sem, r_sem):
-        for peer in tiles:
-            theirs = pl.ds(pl.multiple_of(peer * cap, cap), cap)
-            pltpu.make_async_remote_copy(
-                src_ref=src.at[theirs],
-                dst_ref=dst.at[mine],
-                send_sem=s_sem,
-                recv_sem=r_sem,
-                device_id={"grid": peer},
-            ).start()
-        dst[mine, :] = src[mine, :]
-
-    send_grid(sendx, recvx, fs, fr)
-
-    for k in range(1, M):
-        peer = turn(mi, k, M)
-        pltpu.make_async_remote_copy(
-            src_ref=pred.at[:, pl.ds(pl.multiple_of(peer * LANES, LANES), LANES)],
-            dst_ref=crecv.at[mi],
-            send_sem=cs,
-            recv_sem=cr,
-            device_id={"member": peer},
-        ).start()
-    own_lanes = pl.ds(pl.multiple_of(mi * LANES, LANES), LANES)
-    own_chunk = pltpu.make_async_copy(pred.at[:, own_lanes], crecv.at[mi], own_sem)
-    own_chunk.start()
-
-    for c in loads[7:]:
-        c.wait()
     real = iota((fan, nodes), 0) < ec[...]
     es = jnp.where(real, es_t[...], -1).astype(F32).T.astype(I32)
 
@@ -202,6 +150,59 @@
                     got = lane_gather(table, index[:, cols] + 32 * hh)
                     bias[h // 2, rows_of, cols] = jnp.where(there[:, cols], got, absent)
 
+    for c in range(width // 512):
+        cols = slice(512 * c, 512 * c + 512)
+        ww[core, :, cols] = dot(wep[...], wkv[:, cols]).astype(BF)
+        spread_bias(c * CHUNK)
+    qb[core] = (dot(q[...], wq[...]) * 0.125).astype(BF)
+    for c in range(width // 512, nodes // CHUNK):
+        spread_bias(c * CHUNK)
+
+    for c in loads[10:]:
+        c.wait()
+    pl.semaphore_wait(barrier, G - 1 + M - 1)
+
+    def hand_over(ref, s_sem, r_sem):
+        return pltpu.make_async_remote_copy(
+            src_ref=ref.at[core],
+            dst_ref=ref.at[core],
+            send_sem=s_sem,
+            recv_sem=r_sem,
+            device_id={"member": partner},
+        )
+
+    hand_over(ww, ws, wr).start()
+    hand_over(qb, qs, qr).start()
+
+    mine = pl.ds(pl.multiple_of(gi * cap, cap), cap)
+
+    def send_grid(src, dst, s_sem, r_sem):
+        for peer in tiles:
+            theirs = pl.ds(pl.multiple_of(peer * cap, cap), cap)
+            pltpu.make_async_remote_copy(
+                src_ref=src.at[theirs],
+                dst_ref=dst.at[mine],
+                send_sem=s_sem,
+                recv_sem=r_sem,
+                device_id={"grid": peer},
+            ).start()
+        dst[mine, :] = src[mine, :]
+
+    send_grid(sendx, recvx, fs, fr)
+
+    for k in range(1, M):
+        peer = turn(mi, k, M)
+        pltpu.make_async_remote_copy(
+            src_ref=pred.at[:, pl.ds(pl.multiple_of(peer * LANES, LANES), LANES)],
+            dst_ref=crecv.at[mi],
+            send_sem=cs,
+            recv_sem=cr,
+            device_id={"member": peer},
+        ).start()
+    own_lanes = pl.ds(pl.multiple_of(mi * LANES, LANES), LANES)
+    own_chunk = pltpu.make_async_copy(pred.at[:, own_lanes], crecv.at[mi], own_sem)
+    own_chunk.start()
+
     half = LANES // 2
     for stacked in (qst, ast):
         stacked[...] = jnp.zeros_like(stacked)
@@ -213,8 +214,6 @@
     for c in range(width // 512):
         cols = slice(512 * c, 512 * c + 512)
         grads = dot(cot[0], wo[cols, :], 1, 1).astype(BF)
-        spread_bias(2 * c * CHUNK)
-        spread_bias((2 * c + 1) * CHUNK)
         for k in range(4):
             stack_heads(4 * c + k, grads[:, k * LANES : (k + 1) * LANES], ast)
     wait_bytes(qb.at[0], qr)
@@ -345,8 +344,8 @@
     back = recve[...].T
     high = back.astype(BF)
     terms = jnp.concatenate([high, (back - high.astype(F32)).astype(BF)], axis=0)
-    for c in range(points // 512):
-        cols = slice(512 * c, 512 * c + 512)
+    for c in range(points // 256):
+        cols = slice(256 * c, 256 * c + 256)
         both = dot(terms, sel[:, cols])
         grad[:, 0, cols] = base[:, cols] + (both[:LANES] + both[LANES:])[:variables]
         copy = pltpu.make_async_copy(grad.at[:, :, cols], grad_o.at[:, :, cols], sems.at[2 + c])
@@ -445,7 +444,7 @@
         ),
         in_specs=[vmem_spec] * 5,
         out_specs=(hbm_spec,) * 3,
-        scratch_shapes=[vm((variables, 1, points), F32), vm((1, 1), F32), dma((4,))],
+        scratch_shapes=[vm((variables, 1, points), F32), vm((1, 1), F32), dma((6,))],
         compiler_params=pltpu.CompilerParams(vmem_limit_bytes=16 * 1024 * 1024),
     )(*parts)
     return hidden, jnp.transpose(grad_pred, (1, 0, 2)), loss.reshape(())

time: 33.2 us -> 33.1 us (level)
  no operation moved by 1% of the time
where the time goes in v3:
time: 33.1 us; the launch traced here: 33 us
  Pallas kernels  32.4 us (98%)
  between operations  0.64 us (2%)
    pallas_call x1, Pallas kernels, local(): pl.pallas_call(functools.partial(kernel, G, M), out_shape=(vm((1, nodes,...  30.6 us
    pallas_call x1, Pallas kernels, local(): pl.pallas_call(functools.partial(finish, slots // G), out_shape=(jax.Shap...  1.75 us

profile of v3, /device:TPU:1, one launch (start us, length us, event | category | flops | bytes accessed | tf_op | source)
XLA Modules:
  0.0 33.0 jit_solution(7362869945908994885)
XLA Ops:
  0.6 30.6 %shard_map.148 = (bf16[1,128,1024]{2,1,0:T(8,128)(2,1)S(1)}, f32[100,1024]{1,0:T(8,128)S(1)}, f32[256,128]{1,0:T(8,128)S(1)}, bf16[256,1024]{1,0:T(8,128)(2,1)S(1)}, f32[1,1]{1,0:T(1,128)}) custom-call(f32[100,1,1024]{2,1,0:T(1,128)} %bitcast.7, f32[100,1024]{1,0:T(8,128)} %truth_h.1, f32[1,1024]{1,0:T(1,128)} %bitcast.9, bf16[128,1024]{1,0:T(8,128)(2,1)} %q_h.1, ...), custom_call_target="tpu_custom_call" | custom-call | tf_op jit(solution)/shard_map/pallas_call | solution.py:392
  31.2 1.7 %shard_map.149 = (bf16[1,128,1024]{2,1,0:T(8,128)(2,1)}, f32[100,1,1024]{2,1,0:T(1,128)}, f32[1,1]{1,0:T(1,128)}) custom-call(bf16[1,128,1024]{2,1,0:T(8,128)(2,1)S(1)} %get-tuple-element.11.hid, f32[100,1024]{1,0:T(8,128)S(1)} %get-tuple-element.12.base, f32[256,128]{1,0:T(8,128)S(1)} %get-tuple-element.13.recve, ...), custom_call_target="tpu_custom_call" | custom-call | tf_op jit(solution)/shard_map/pallas_call | solution.py:438

commit v4 on v2

--- a/solution.py
+++ b/solution.py
@@ -9,6 +9,7 @@
 
 alpha_fair = 0.95
 absent = -1e30
+log2e = 1.4426950408889634
 steep = 3e38
 
 BF = jnp.bfloat16
@@ -129,6 +130,8 @@
         ww[core, :, cols] = dot(wep[...], wkv[:, cols]).astype(BF)
     qb[core] = (dot(q[...], wq[...]) * 0.125).astype(BF)
 
+    for c in loads[7:]:
+        c.wait()
     pl.semaphore_wait(barrier, G - 1 + M - 1)
 
     def hand_over(ref, s_sem, r_sem):
@@ -172,8 +175,6 @@
     own_chunk = pltpu.make_async_copy(pred.at[:, own_lanes], crecv.at[mi], own_sem)
     own_chunk.start()
 
-    for c in loads[7:]:
-        c.wait()
     real = iota((fan, nodes), 0) < ec[...]
     es = jnp.where(real, es_t[...], -1).astype(F32).T.astype(I32)
 
@@ -186,7 +187,7 @@
             inverse = jnp.where(edges[:, e : e + 1] == slot_ids, e, inverse)
         there = inverse >= 0
         index = jnp.maximum(inverse, 0)
-        columns = [eb[r, j * LANES : (j + 1) * LANES] for j in range(4)]
+        columns = [eb[r, j * LANES : (j + 1) * LANES] * log2e for j in range(4)]
         l = iota((CHUNK, LANES), 1)
         edge = l & (fan - 1)
         for t in range(4):
@@ -200,7 +201,9 @@
                 for side in range(slots // LANES):
                     cols = slice(side * LANES, (side + 1) * LANES)
                     got = lane_gather(table, index[:, cols] + 32 * hh)
-                    bias[h // 2, rows_of, cols] = jnp.where(there[:, cols], got, absent)
+                    bias[h // 2, rows_of, cols] = jnp.where(
+                        there[:, cols], got, absent
+                    )
 
     half = LANES // 2
     for stacked in (qst, ast):
@@ -223,11 +226,11 @@
         lanes = slice(p * LANES, (p + 1) * LANES)
         inner = slice((p % 4) * LANES, (p % 4 + 1) * LANES)
         stack_heads(p, qb[p // 4, :, inner], qst)
-        for stacked, weights, by_node, by_field in (
-            (qst, ww[0, :, lanes], qw, qw_t),
-            (ast, ww[1, :, lanes], aw, aw_t),
+        for stacked, weights, by_node, by_field, factor in (
+            (qst, ww[0, :, lanes], qw, qw_t, log2e),
+            (ast, ww[1, :, lanes], aw, aw_t, 1.0),
         ):
-            by_node[p] = dot(stacked[p], weights, 1, 1).astype(BF)
+            by_node[p] = (dot(stacked[p], weights, 1, 1) * factor).astype(BF)
             by_field[p] = dot(weights, stacked[p], 1, 1).astype(BF)
 
     wait_bytes(recvx.at[pl.ds(0, slots - cap)], fr)
@@ -294,10 +297,10 @@
             statistics()
         if p + 1 < pairs:
             products(p + 1)
-        for i in range(2):
-            r = slice(i * nodes, (i + 1) * nodes)
+        for i in range(2 * nodes // 64):
+            r = slice(i * 64, (i + 1) * 64)
             s = s_scr[p, r, :] + bias[p, r, :]
-            e = jnp.exp(s - jnp.max(s, axis=1, keepdims=True))
+            e = jnp.exp2(s - jnp.max(s, axis=1, keepdims=True))
             g = g_scr[p, r, :]
             share = 1.0 / jnp.sum(e, axis=1, keepdims=True)
             inner = jnp.sum(e * g, axis=1, keepdims=True) * share

time: 33.2 us -> 33.2 us (level)
  no operation moved by 1% of the time
where the time goes in v4:
time: 33.2 us; the launch traced here: 33.1 us
  Pallas kernels  32.4 us (98%)
  between operations  0.64 us (2%)
    pallas_call x1, Pallas kernels, local(): pl.pallas_call(functools.partial(kernel, G, M), out_shape=(vm((1, nodes,...  30.7 us
    pallas_call x1, Pallas kernels, local(): pl.pallas_call(functools.partial(finish, slots // G), out_shape=(jax.Shap...  1.71 us

profile of v4, /device:TPU:1, one launch (start us, length us, event | category | flops | bytes accessed | tf_op | source)
XLA Modules:
  0.0 33.1 jit_solution(11227622335196256222)
XLA Ops:
  0.6 30.7 %shard_map.148 = (bf16[1,128,1024]{2,1,0:T(8,128)(2,1)S(1)}, f32[100,1024]{1,0:T(8,128)S(1)}, f32[256,128]{1,0:T(8,128)S(1)}, bf16[256,1024]{1,0:T(8,128)(2,1)S(1)}, f32[1,1]{1,0:T(1,128)}) custom-call(f32[100,1,1024]{2,1,0:T(1,128)} %bitcast.7, f32[100,1024]{1,0:T(8,128)} %truth_h.1, f32[1,1024]{1,0:T(1,128)} %bitcast.9, bf16[128,1024]{1,0:T(8,128)(2,1)} %q_h.1, ...), custom_call_target="tpu_custom_call" | custom-call | tf_op jit(solution)/shard_map/pallas_call | solution.py:396
  31.3 1.7 %shard_map.149 = (bf16[1,128,1024]{2,1,0:T(8,128)(2,1)}, f32[100,1,1024]{2,1,0:T(1,128)}, f32[1,1]{1,0:T(1,128)}) custom-call(bf16[1,128,1024]{2,1,0:T(8,128)(2,1)S(1)} %get-tuple-element.11.hid, f32[100,1024]{1,0:T(8,128)S(1)} %get-tuple-element.12.base, f32[256,128]{1,0:T(8,128)S(1)} %get-tuple-element.13.recve, ...), custom_call_target="tpu_custom_call" | custom-call | tf_op jit(solution)/shard_map/pallas_call | solution.py:442

commit v5 on v4

--- a/solution.py
+++ b/solution.py
@@ -122,59 +122,8 @@
     sendx[...] = jnp.where(lane == variables, tile_area, x)
 
 
-    for c in loads[4:7]:
+    for c in loads[4:]:
         c.wait()
-    wep[0:variables, :] = we[...]
-    for c in range(width // 512):
-        cols = slice(512 * c, 512 * c + 512)
-        ww[core, :, cols] = dot(wep[...], wkv[:, cols]).astype(BF)
-    qb[core] = (dot(q[...], wq[...]) * 0.125).astype(BF)
-
-    for c in loads[7:]:
-        c.wait()
-    pl.semaphore_wait(barrier, G - 1 + M - 1)
-
-    def hand_over(ref, s_sem, r_sem):
-        return pltpu.make_async_remote_copy(
-            src_ref=ref.at[core],
-            dst_ref=ref.at[core],
-            send_sem=s_sem,
-            recv_sem=r_sem,
-            device_id={"member": partner},
-        )
-
-    hand_over(ww, ws, wr).start()
-    hand_over(qb, qs, qr).start()
-
-    mine = pl.ds(pl.multiple_of(gi * cap, cap), cap)
-
-    def send_grid(src, dst, s_sem, r_sem):
-        for peer in tiles:
-            theirs = pl.ds(pl.multiple_of(peer * cap, cap), cap)
-            pltpu.make_async_remote_copy(
-                src_ref=src.at[theirs],
-                dst_ref=dst.at[mine],
-                send_sem=s_sem,
-                recv_sem=r_sem,
-                device_id={"grid": peer},
-            ).start()
-        dst[mine, :] = src[mine, :]
-
-    send_grid(sendx, recvx, fs, fr)
-
-    for k in range(1, M):
-        peer = turn(mi, k, M)
-        pltpu.make_async_remote_copy(
-            src_ref=pred.at[:, pl.ds(pl.multiple_of(peer * LANES, LANES), LANES)],
-            dst_ref=crecv.at[mi],
-            send_sem=cs,
-            recv_sem=cr,
-            device_id={"member": peer},
-        ).start()
-    own_lanes = pl.ds(pl.multiple_of(mi * LANES, LANES), LANES)
-    own_chunk = pltpu.make_async_copy(pred.at[:, own_lanes], crecv.at[mi], own_sem)
-    own_chunk.start()
-
     real = iota((fan, nodes), 0) < ec[...]
     es = jnp.where(real, es_t[...], -1).astype(F32).T.astype(I32)
 
@@ -205,6 +154,58 @@
                         there[:, cols], got, absent
                     )
 
+    for c in range(2):
+        spread_bias(c * CHUNK)
+
+    pl.semaphore_wait(barrier, G - 1 + M - 1)
+    for k in range(1, M):
+        peer = turn(mi, k, M)
+        pltpu.make_async_remote_copy(
+            src_ref=pred.at[:, pl.ds(pl.multiple_of(peer * LANES, LANES), LANES)],
+            dst_ref=crecv.at[mi],
+            send_sem=cs,
+            recv_sem=cr,
+            device_id={"member": peer},
+        ).start()
+    own_lanes = pl.ds(pl.multiple_of(mi * LANES, LANES), LANES)
+    own_chunk = pltpu.make_async_copy(pred.at[:, own_lanes], crecv.at[mi], own_sem)
+    own_chunk.start()
+
+    mine = pl.ds(pl.multiple_of(gi * cap, cap), cap)
+
+    def send_grid(src, dst, s_sem, r_sem):
+        for peer in tiles:
+            theirs = pl.ds(pl.multiple_of(peer * cap, cap), cap)
+            pltpu.make_async_remote_copy(
+                src_ref=src.at[theirs],
+                dst_ref=dst.at[mine],
+                send_sem=s_sem,
+                recv_sem=r_sem,
+                device_id={"grid": peer},
+            ).start()
+        dst[mine, :] = src[mine, :]
+
+    send_grid(sendx, recvx, fs, fr)
+
+    wep[0:variables, :] = we[...]
+    for c in range(width // 512):
+        cols = slice(512 * c, 512 * c + 512)
+        ww[core, :, cols] = dot(wep[...], wkv[:, cols]).astype(BF)
+    qb[core] = (dot(q[...], wq[...]) * 0.125).astype(BF)
+
+    def hand_over(ref, s_sem, r_sem):
+        return pltpu.make_async_remote_copy(
+            src_ref=ref.at[core],
+            dst_ref=ref.at[core],
+            send_sem=s_sem,
+            recv_sem=r_sem,
+            device_id={"member": partner},
+        )
+
+    hand_over(ww, ws, wr).start()
+    hand_over(qb, qs, qr).start()
+
+
     half = LANES // 2
     for stacked in (qst, ast):
         stacked[...] = jnp.zeros_like(stacked)
@@ -216,8 +217,7 @@
     for c in range(width // 512):
         cols = slice(512 * c, 512 * c + 512)
         grads = dot(cot[0], wo[cols, :], 1, 1).astype(BF)
-        spread_bias(2 * c * CHUNK)
-        spread_bias((2 * c + 1) * CHUNK)
+        spread_bias((2 + c) * CHUNK)
         for k in range(4):
             stack_heads(4 * c + k, grads[:, k * LANES : (k + 1) * LANES], ast)
     wait_bytes(qb.at[0], qr)
@@ -293,7 +293,7 @@
 
     products(0)
     for p in range(pairs):
-        if p == 5:
+        if p == 3:
             statistics()
         if p + 1 < pairs:
             products(p + 1)

time: 33.2 us -> 32 us (0.964)
  Pallas kernels: 32.4 us -> 31.3 us
    pallas_call x1, Pallas kernels: 30.7 us -> 29.6 us  [local(): pl.pallas_call(functools.partial(kernel, G, M), out_shape=(vm((1, nodes,...]
where the time goes in v5:
time: 32 us; the launch traced here: 31.9 us
  Pallas kernels  31.3 us (98%)
  between operations  0.64 us (2%)
    pallas_call x1, Pallas kernels, local(): pl.pallas_call(functools.partial(kernel, G, M), out_shape=(vm((1, nodes,...  29.6 us
    pallas_call x1, Pallas kernels, local(): pl.pallas_call(functools.partial(finish, slots // G), out_shape=(jax.Shap...  1.71 us

profile of v5, /device:TPU:1, one launch (start us, length us, event | category | flops | bytes accessed | tf_op | source)
XLA Modules:
  0.0 31.9 jit_solution(3546688844907542720)
XLA Ops:
  0.6 29.6 %shard_map.148 = (bf16[1,128,1024]{2,1,0:T(8,128)(2,1)S(1)}, f32[100,1024]{1,0:T(8,128)S(1)}, f32[256,128]{1,0:T(8,128)S(1)}, bf16[256,1024]{1,0:T(8,128)(2,1)S(1)}, f32[1,1]{1,0:T(1,128)}) custom-call(f32[100,1,1024]{2,1,0:T(1,128)} %bitcast.7, f32[100,1024]{1,0:T(8,128)} %truth_h.1, f32[1,1024]{1,0:T(1,128)} %bitcast.9, bf16[128,1024]{1,0:T(8,128)(2,1)} %q_h.1, ...), custom_call_target="tpu_custom_call" | custom-call | tf_op jit(solution)/shard_map/pallas_call | solution.py:396
  30.2 1.7 %shard_map.149 = (bf16[1,128,1024]{2,1,0:T(8,128)(2,1)}, f32[100,1,1024]{2,1,0:T(1,128)}, f32[1,1]{1,0:T(1,128)}) custom-call(bf16[1,128,1024]{2,1,0:T(8,128)(2,1)S(1)} %get-tuple-element.11.hid, f32[100,1024]{1,0:T(8,128)S(1)} %get-tuple-element.12.base, f32[256,128]{1,0:T(8,128)S(1)} %get-tuple-element.13.recve, ...), custom_call_target="tpu_custom_call" | custom-call | tf_op jit(solution)/shard_map/pallas_call | solution.py:442

commit v6 on v5

--- a/solution.py
+++ b/solution.py
@@ -76,12 +76,12 @@
     partner = mi + 1 - 2 * core
     wq_h = wq_h.at[:, pl.ds(pl.multiple_of(core * (width // 2), LANES), width // 2)]
     wkv_h = wkv_h.at[:, pl.ds(pl.multiple_of(core * width, LANES), width)]
-    sources = [sr_h, pred_h, area_h, we_h, wkv_h, q_h, wq_h, es_h, ec_h, eb_h, cot_h, wo_h, truth_h]
-    targets = [sr, predl, area, we, wkv, q, wq, es_t, ec, eb, cot, wo, truth]
+    sources = [sr_h, pred_h, area_h, es_h, ec_h, eb_h, we_h, wkv_h, q_h, wq_h, cot_h, wo_h, truth_h]
+    targets = [sr, predl, area, es_t, ec, eb, we, wkv, q, wq, cot, wo, truth]
     loads = [
         pltpu.make_async_copy(s, t, ld_sem.at[i]) for i, (s, t) in enumerate(zip(sources, targets))
     ]
-    for c in loads[:4]:
+    for c in loads[:6]:
         c.start()
 
     barrier = pltpu.get_barrier_semaphore()
@@ -98,7 +98,7 @@
         pl.semaphore_signal(barrier, inc=1, device_id={"grid": peer})
     for k in range(1, M):
         pl.semaphore_signal(barrier, inc=1, device_id={"member": turn(mi, k, M)})
-    for c in loads[4:]:
+    for c in loads[6:]:
         c.start()
 
     loads[0].wait()
@@ -111,7 +111,7 @@
         sel[r, :] = jnp.where(hit, 1.0, 0.0).astype(BF)
     predp[...] = jnp.zeros_like(predp)
     wep[...] = jnp.zeros_like(wep)
-    for c in loads[1:4]:
+    for c in loads[1:6]:
         c.wait()
     pred[...] = predl[:, 0, :]
     predp[0:variables, :] = pred[...].astype(BF)
@@ -119,11 +119,7 @@
     lane = iota((slots, LANES), 1)
     sub = iota((slots, LANES), 0)
     x = dot(sel[...], predp[...], 1, 1)
-    sendx[...] = jnp.where(lane == variables, tile_area, x)
-
-
-    for c in loads[4:]:
-        c.wait()
+
     real = iota((fan, nodes), 0) < ec[...]
     es = jnp.where(real, es_t[...], -1).astype(F32).T.astype(I32)
 
@@ -157,6 +153,11 @@
     for c in range(2):
         spread_bias(c * CHUNK)
 
+    sendx[...] = jnp.where(lane == variables, tile_area, x)
+
+
+    for c in loads[6:]:
+        c.wait()
     pl.semaphore_wait(barrier, G - 1 + M - 1)
     for k in range(1, M):
         peer = turn(mi, k, M)
@@ -187,12 +188,6 @@
 
     send_grid(sendx, recvx, fs, fr)
 
-    wep[0:variables, :] = we[...]
-    for c in range(width // 512):
-        cols = slice(512 * c, 512 * c + 512)
-        ww[core, :, cols] = dot(wep[...], wkv[:, cols]).astype(BF)
-    qb[core] = (dot(q[...], wq[...]) * 0.125).astype(BF)
-
     def hand_over(ref, s_sem, r_sem):
         return pltpu.make_async_remote_copy(
             src_ref=ref.at[core],
@@ -202,7 +197,13 @@
             device_id={"member": partner},
         )
 
+    wep[0:variables, :] = we[...]
+    for c in range(width // 512):
+        cols = slice(512 * c, 512 * c + 512)
+        ww[core, :, cols] = dot(wep[...], wkv[:, cols]).astype(BF)
     hand_over(ww, ws, wr).start()
+    qb[core] = (dot(q[...], wq[...]) * 0.125).astype(BF)
+
     hand_over(qb, qs, qr).start()
 
 

time: 32 us -> 32.9 us (1.028)
  Pallas kernels: 31.3 us -> 32.1 us
    pallas_call x1, Pallas kernels: 29.6 us -> 30.4 us  [local(): pl.pallas_call(functools.partial(kernel, G, M), out_shape=(vm((1, nodes,...]
where the time goes in v6:
time: 32.9 us; the launch traced here: 32.8 us
  Pallas kernels  32.1 us (98%)
  between operations  0.64 us (2%)
    pallas_call x1, Pallas kernels, local(): pl.pallas_call(functools.partial(kernel, G, M), out_shape=(vm((1, nodes,...  30.4 us
    pallas_call x1, Pallas kernels, local(): pl.pallas_call(functools.partial(finish, slots // G), out_shape=(jax.Shap...  1.71 us

profile of v6, /device:TPU:1, one launch (start us, length us, event | category | flops | bytes accessed | tf_op | source)
XLA Modules:
  0.0 32.8 jit_solution(1051051037726038327)
XLA Ops:
  0.6 30.4 %shard_map.148 = (bf16[1,128,1024]{2,1,0:T(8,128)(2,1)S(1)}, f32[100,1024]{1,0:T(8,128)S(1)}, f32[256,128]{1,0:T(8,128)S(1)}, bf16[256,1024]{1,0:T(8,128)(2,1)S(1)}, f32[1,1]{1,0:T(1,128)}) custom-call(f32[100,1,1024]{2,1,0:T(1,128)} %bitcast.7, f32[100,1024]{1,0:T(8,128)} %truth_h.1, f32[1,1024]{1,0:T(1,128)} %bitcast.9, bf16[128,1024]{1,0:T(8,128)(2,1)} %q_h.1, ...), custom_call_target="tpu_custom_call" | custom-call | tf_op jit(solution)/shard_map/pallas_call | solution.py:397
  31.1 1.7 %shard_map.149 = (bf16[1,128,1024]{2,1,0:T(8,128)(2,1)}, f32[100,1,1024]{2,1,0:T(1,128)}, f32[1,1]{1,0:T(1,128)}) custom-call(bf16[1,128,1024]{2,1,0:T(8,128)(2,1)S(1)} %get-tuple-element.11.hid, f32[100,1024]{1,0:T(8,128)S(1)} %get-tuple-element.12.base, f32[256,128]{1,0:T(8,128)S(1)} %get-tuple-element.13.recve, ...), custom_call_target="tpu_custom_call" | custom-call | tf_op jit(solution)/shard_map/pallas_call | solution.py:443
